TPU v7x, 256 devices: a whole 4x4x8 slice. The times are simulated.
256 devices in a mesh: layer: 8 (over x, z_hi), latent: 8 (over z_lo, core), token: 4 (over y).
Axes of the slice: x: 4, y: 4, z: 8 (z_hi: 2, z_lo: 4; z = z_hi * 4 + z_lo), core: 2. Of those that a mesh axis runs over, the one named last changes fastest.
Arguments:
- streams: bfloat16 [8, 4096, 8192], P('layer', 'token', 'latent'), may hold values from -6 to 6
- active_latents: int32 [4096, 64], P('token'), may hold values from 0 to 383, all different within a row
- enc_weight: float32 [8, 384, 8192], P('layer', 'latent', 'token'), may hold values from -6 to 6
- enc_moment: float32 [8, 384, 8192], P('layer', 'latent', 'token'), may hold values from -0.0029296875 to 0.0029296875
- enc_second: float32 [8, 384, 8192], P('layer', 'latent', 'token'), may hold values from 1e-09 to 1e-07
- dec_weight: float32 [8, 384, 8192], P('layer', 'latent', 'token'), may hold values from -6 to 6
- dec_moment: float32 [8, 384, 8192], P('layer', 'latent', 'token'), may hold values from -0.0029296875 to 0.0029296875
- dec_second: float32 [8, 384, 8192], P('layer', 'latent', 'token'), may hold values from 1e-09 to 1e-07
Outputs:
- enc_weight_new: float32 [8, 384, 8192], P('layer', 'latent', 'token')
- enc_moment_new: float32 [8, 384, 8192], P('layer', 'latent', 'token')
- enc_second_new: float32 [8, 384, 8192], P('layer', 'latent', 'token')
- dec_weight_new: float32 [8, 384, 8192], P('layer', 'latent', 'token')
- dec_moment_new: float32 [8, 384, 8192], P('layer', 'latent', 'token')
- dec_second_new: float32 [8, 384, 8192], P('layer', 'latent', 'token')
Inputs may be any that keep to these rules, and one draw needn't show every extreme that they name: `active_latents`: each row names 64 different latents; every latent is named by some row.
All inputs are finite; a program needn't handle non-finite values.
Results may differ from a plain program's by a relative error of at most 0.0056.
Values may be sent and summed in bfloat16 or wider, within the bound.
No kernel may reach another device: no remote copies, remote signals or barrier semaphores. Data moves between devices by JAX's collectives and lax.ppermute only.
A program may use at most 64 MiB of HBM per device.

v0:
```python
import math
import jax
import jax.numpy as jnp
from jax import lax
from jax.sharding import PartitionSpec as P

K = 64
ADAM_STEP = 100


def adam_step(weight, moment, second, gradient):
    moment_new = 0.9 * moment + 0.1 * gradient
    second_new = 0.999 * second + 0.001 * gradient * gradient
    first_fix = 1.0 - 0.9**ADAM_STEP
    second_fix = 1.0 - 0.999**ADAM_STEP
    weight_new = weight - 0.2 * (moment_new / first_fix) / (
        jnp.sqrt(second_new / second_fix) + 1e-08
    )
    return (weight_new, moment_new, second_new)


def contract(left, right, left_dim, right_dim):
    return lax.dot_general(
        left, right, (((left_dim,), (right_dim,)), ((), ())), preferred_element_type=jnp.float32
    )


def matches(active_latents, total_lat):
    latent_ids = jnp.arange(total_lat, dtype=jnp.int32)[None, None, :]
    return active_latents[:, :, None] == latent_ids


def masked_total(partial_value, selected):
    summed = lax.psum(partial_value, ("layer", "latent"))
    return (summed * selected).astype(jnp.bfloat16)


def body(
    streams, active_latents, enc_weight, enc_moment, enc_second, dec_weight, dec_moment, dec_second
):
    tok_rows = streams.shape[1]
    lat_dev = enc_weight.shape[1]
    n_layer = lax.axis_size("layer")
    total_lat = lat_dev * lax.axis_size("latent")
    features = enc_weight.shape[2] * lax.axis_size("token")
    tokens_all = tok_rows * lax.axis_size("token")
    enc_scale = 1.0 / math.sqrt(n_layer * features)
    dec_scale = 1.0 / math.sqrt(K)
    casted = (enc_weight[0].astype(jnp.bfloat16), dec_weight[0].astype(jnp.bfloat16))
    gathered = (
        lax.all_gather(casted[0], "token", axis=1, tiled=True),
        lax.all_gather(casted[1], "token", axis=1, tiled=True),
    )
    enc_cols, dec_cols = (
        lax.all_to_all(gathered[0], "latent", split_axis=1, concat_axis=0, tiled=True),
        lax.all_to_all(gathered[1], "latent", split_axis=1, concat_axis=0, tiled=True),
    )
    own_rows = streams[0]
    selected = jnp.sum(matches(active_latents, total_lat).astype(jnp.float32), axis=1)
    pre_partial = contract(own_rows, enc_cols, 1, 1) * enc_scale
    latent_codes = masked_total(pre_partial, selected)
    rebuilt = jnp.dot(latent_codes, dec_cols, preferred_element_type=jnp.float32) * dec_scale
    errors = (rebuilt - own_rows.astype(jnp.float32)).astype(jnp.bfloat16)
    back_partial = contract(errors, dec_cols, 1, 1) * dec_scale
    backward = masked_total(back_partial, selected)
    dec_partial = contract(latent_codes, errors, 0, 0) * (dec_scale / tokens_all)
    enc_partial = contract(backward, own_rows, 0, 0) * (enc_scale / tokens_all)
    exchanged = (
        lax.all_to_all(enc_partial, "latent", split_axis=0, concat_axis=1, tiled=True),
        lax.all_to_all(dec_partial, "latent", split_axis=0, concat_axis=1, tiled=True),
    )
    enc_grad, dec_grad = (
        lax.psum_scatter(exchanged[0], "token", scatter_dimension=1, tiled=True),
        lax.psum_scatter(exchanged[1], "token", scatter_dimension=1, tiled=True),
    )
    enc_out = adam_step(enc_weight[0], enc_moment[0], enc_second[0], enc_grad)
    dec_out = adam_step(dec_weight[0], dec_moment[0], dec_second[0], dec_grad)
    return (
        enc_out[0][None],
        enc_out[1][None],
        enc_out[2][None],
        dec_out[0][None],
        dec_out[1][None],
        dec_out[2][None],
    )


def solution(mesh):
    in_specs = (
        P("layer", "token", "latent"),
        P("token", None),
        P("layer", "latent", "token"),
        P("layer", "latent", "token"),
        P("layer", "latent", "token"),
        P("layer", "latent", "token"),
        P("layer", "latent", "token"),
        P("layer", "latent", "token"),
    )
    out_specs = (
        P("layer", "latent", "token"),
        P("layer", "latent", "token"),
        P("layer", "latent", "token"),
        P("layer", "latent", "token"),
        P("layer", "latent", "token"),
        P("layer", "latent", "token"),
    )
    return jax.shard_map(body, mesh=mesh, in_specs=in_specs, out_specs=out_specs, check_vma=False)
```

profile of v0, /device:TPU:2, one launch (start us, length us, event | category | flops | bytes accessed | tf_op | source)
XLA Modules:
  0.0 534.7 jit_solution(17642249158765734346)
XLA Ops:
  7.2 1.0 bitcast_convert_fusion.1
  8.2 13.8 %all_gather.6 = bf16[48,8192]{1,0:T(8,128)(2,1)S(1)} all-gather(bf16[48,2048]{1,0:T(8,128)(2,1)S(1)} %bitcast_convert_fusion.1), channel_id=1, replica_groups=mesh['layer'=8,'latent'=8,'token'=4] {'token'}, dimensions={1}, use_global_device_ids=true | all-gather | bytes 983040 | tf_op jit(solution)/shard_map/all_gather | solution.py:51
  22.0 0.0 copy-start.8
  22.0 1.0 copy.42
  23.0 0.0 copy-start.2
  23.0 6.0 %all-to-all-start = ((bf16[48,8,1024]{2,0,1:T(8,128)(2,1)}), bf16[48,8,1024]{2,0,1:T(8,128)(2,1)}, u32[]{:S(2)}, u32[]{:S(2)}) async-start(bf16[48,8,1024]{2,0,1:T(8,128)(2,1)} %bitcast.84), calls=%async_computation | async-start | bytes 1572864 | tf_op jit(solution)/shard_map/all_to_all | solution.py:55
  29.0 0.0 copy-done.8
  29.0 0.2 copy.31
  29.2 0.0 copy-done.2
  29.3 14.4 %all_gather.7 = bf16[48,8192]{1,0:T(8,128)(2,1)S(1)} all-gather(bf16[48,2048]{1,0:T(8,128)(2,1)S(1)} %bitcast_convert_fusion), channel_id=1, replica_groups=mesh['layer'=8,'latent'=8,'token'=4] {'token'}, dimensions={1}, use_global_device_ids=true | all-gather | bytes 983040 | tf_op jit(solution)/shard_map/all_gather | solution.py:52
  43.7 0.0 copy-start
  43.7 1.0 copy.41
  44.7 5.4 %all-to-all-done = bf16[48,8,1024]{2,0,1:T(8,128)(2,1)} async-done(((bf16[48,8,1024]{2,0,1:T(8,128)(2,1)}), bf16[48,8,1024]{2,0,1:T(8,128)(2,1)}, u32[]{:S(2)}, u32[]{:S(2)}) %all-to-all-start) | async-done | bytes 786464 | tf_op jit(solution)/shard_map/all_to_all | solution.py:55
  50.1 4.2 all-to-all-start.1
  54.3 0.0 all-reduce.3.cloned.1.call-start
  54.4 0.0 copy-done
  54.4 3.5 fusion.4
  57.9 0.0 all-reduce.3.cloned.1.call-update
  58.0 17.8 %convert_reduce_fusion = f32[1024,384]{1,0:T(8,128)S(1)} fusion(s32[1024,64]{1,0:T(8,128)S(1)} %copy.31), kind=kLoop, calls=%fused_computation | loop fusion | flops 75104256 | bytes 1835008 | tf_op jit(solution)/shard_map/reduce_sum | solution.py:59
  75.8 172.1 %all-reduce.3.cloned.1.call-done = f32[1024,384]{1,0:T(8,128)} async-done(((f32[1024,384]{1,0:T(8,128)}), f32[1024,384]{1,0:T(8,128)}) %all-reduce.3.cloned.1.call-update) | async-done | bytes 1572880 | tf_op jit(solution)/shard_map/psum | solution.py:34
  247.8 1.6 multiply_convert_fusion.1
  249.4 0.0 all-to-all-done.1
  249.4 3.1 subtract_convert_fusion
  252.5 0.0 copy-start.1
  252.5 2.1 convolution_multiply_fusion
  254.7 0.0 copy-done.1
  254.7 3.6 all-to-all-start.3
  258.2 0.0 all-reduce.5.cloned.1.call-start
  258.3 4.2 convolution_multiply_fusion.1
  262.5 0.0 all-reduce.5.cloned.1.call-update
  262.5 0.0 reduce-scatter.5.cloned.1.call-start
  262.6 35.6 %all-to-all-done.3 = f32[8,48,1024]{2,1,0:T(8,128)S(1)} async-done(((f32[8,48,1024]{2,1,0:T(8,128)}), f32[8,48,1024]{2,1,0:T(8,128)S(1)}, u32[]{:S(2)}, u32[]{:S(2)}) %all-to-all-start.3) | async-done | bytes 1572896 | tf_op jit(solution)/shard_map/all_to_all | solution.py:70
  298.2 1.2 copy.38
  299.5 0.0 reduce-scatter.5.cloned.1.call-update
  299.5 0.0 reduce-scatter.3.cloned.1.call-start
  299.5 154.2 %all-reduce.5.cloned.1.call-done = f32[1024,384]{1,0:T(8,128)} async-done(((f32[1024,384]{1,0:T(8,128)}), f32[1024,384]{1,0:T(8,128)}) %all-reduce.5.cloned.1.call-update) | async-done | bytes 1572880 | tf_op jit(solution)/shard_map/psum | solution.py:34
  453.8 3.1 fusion.7
  456.8 40.9 %all_to_all.76 = f32[8,48,1024]{2,1,0:T(8,128)S(1)} all-to-all(f32[8,48,1024]{2,1,0:T(8,128)S(1)} %bitcast.90), channel_id=1, replica_groups=mesh['layer'=8,'latent'=8,'token'=4] {'latent'}, dimensions={0} | all-to-all | bytes 3145728 | tf_op jit(solution)/shard_map/all_to_all | solution.py:69
  497.7 1.3 copy.37
  499.0 0.0 copy-start.4
  499.0 0.0 copy-start.5
  499.1 0.0 reduce-scatter.3.cloned.1.call-update
  499.1 0.0 copy-start.3
  499.1 0.0 copy-start.6
  499.1 0.0 copy-start.7
  499.1 0.0 reduce-scatter.5.cloned.1.call-done
  499.1 0.9 copy-done.4
  500.0 0.1 copy-done.5
  500.2 2.2 fusion.16
  502.4 23.5 %reduce-scatter.3.cloned.1.call-done = f32[48,2048]{1,0:T(8,128)} async-done(((f32[48,8192]{1,0:T(8,128)}), f32[48,2048]{1,0:T(8,128)}) %reduce-scatter.3.cloned.1.call-update) | async-done | bytes 393232 | tf_op jit(solution)/shard_map/reduce_scatter | solution.py:73
  525.9 0.0 copy-done.3
  525.9 0.0 copy-done.6
  525.9 0.0 copy-done.7
  525.9 2.3 fusion.17
  (1 shorter events, 0.0 us)
Async XLA Ops:
  22.0 7.0 %copy-start.8 = (s32[1024,64]{0,1:T(8,128)S(1)}, s32[1024,64]{0,1:T(8,128)}, u32[]{:S(2)}) copy-start(s32[1024,64]{0,1:T(8,128)} %param.9) | copy-start | bytes 786436
  23.0 6.2 %copy-start.2 = (f32[1,48,2048]{2,1,0:T(8,128)S(1)}, f32[1,48,2048]{2,1,0:T(8,128)}, u32[]{:S(2)}) copy-start(f32[1,48,2048]{2,1,0:T(8,128)} %param.13) | copy-start | bytes 1179652
  23.0 27.1 %all-to-all-start = ((bf16[48,8,1024]{2,0,1:T(8,128)(2,1)}), bf16[48,8,1024]{2,0,1:T(8,128)(2,1)}, u32[]{:S(2)}, u32[]{:S(2)}) async-start(bf16[48,8,1024]{2,0,1:T(8,128)(2,1)} %bitcast.84), calls=%async_computation | async-start | bytes 1572864 | tf_op jit(solution)/shard_map/all_to_all | solution.py:55
  43.7 10.7 %copy-start = (bf16[1,1024,1024]{2,1,0:T(8,128)(2,1)S(1)}, bf16[1,1024,1024]{2,1,0:T(8,128)(2,1)}, u32[]{:S(2)}) copy-start(bf16[1,1024,1024]{2,1,0:T(8,128)(2,1)} %param.8) | copy-start | bytes 6291460
  50.1 199.3 %all-to-all-start.1 = ((bf16[48,8,1024]{2,0,1:T(8,128)(2,1)}), bf16[48,8,1024]{2,0,1:T(8,128)(2,1)}, u32[]{:S(2)}, u32[]{:S(2)}) async-start(bf16[48,8,1024]{2,0,1:T(8,128)(2,1)} %bitcast.83), calls=%async_computation.1 | async-start | bytes 1572864 | tf_op jit(solution)/shard_map/all_to_all | solution.py:56
  54.3 193.5 %all-reduce.3.cloned.1.call-start = ((), (), s32[]{:S(2)}) async-start(), calls=%async_computation.6 | async-start | bytes 3145728 | tf_op jit(solution)/shard_map/psum | solution.py:34
  252.5 2.2 copy-start.1
  254.7 43.6 %all-to-all-start.3 = ((f32[8,48,1024]{2,1,0:T(8,128)}), f32[8,48,1024]{2,1,0:T(8,128)S(1)}, u32[]{:S(2)}, u32[]{:S(2)}) async-start(f32[8,48,1024]{2,1,0:T(8,128)} %bitcast.87), calls=%async_computation.4 | async-start | bytes 3145728 | tf_op jit(solution)/shard_map/all_to_all | solution.py:70
  258.2 195.5 %all-reduce.5.cloned.1.call-start = ((), (), s32[]{:S(2)}) async-start(), calls=%async_computation.7 | async-start | bytes 3145728 | tf_op jit(solution)/shard_map/psum | solution.py:34
  262.5 236.6 %reduce-scatter.5.cloned.1.call-start = ((), (), s32[]{:S(2)}) async-start(), calls=%async_computation.9 | async-start | bytes 1966080 | tf_op jit(solution)/shard_map/reduce_scatter | solution.py:74
  299.5 226.4 %reduce-scatter.3.cloned.1.call-start = ((), (), s32[]{:S(2)}) async-start(), calls=%async_computation.8 | async-start | bytes 1966080 | tf_op jit(solution)/shard_map/reduce_scatter | solution.py:73
  499.0 1.0 copy-start.4
  499.0 1.1 copy-start.5
  499.1 26.9 %copy-start.3 = (f32[1,48,2048]{2,1,0:T(8,128)S(1)}, f32[1,48,2048]{2,1,0:T(8,128)}, u32[]{:S(2)}) copy-start(f32[1,48,2048]{2,1,0:T(8,128)} %param.10) | copy-start | bytes 1179652
  499.1 26.8 %copy-start.6 = (f32[1,48,2048]{2,1,0:T(8,128)S(1)}, f32[1,48,2048]{2,1,0:T(8,128)}, u32[]{:S(2)}) copy-start(f32[1,48,2048]{2,1,0:T(8,128)} %param.12) | copy-start | bytes 1179652
  499.1 26.8 %copy-start.7 = (f32[1,48,2048]{2,1,0:T(8,128)S(1)}, f32[1,48,2048]{2,1,0:T(8,128)}, u32[]{:S(2)}) copy-start(f32[1,48,2048]{2,1,0:T(8,128)} %param.11) | copy-start | bytes 1179652
Sparse Core Ops, SparseCore 0:
  58.6 189.2 all-reduce.2
  262.7 191.0 all-reduce.4
  456.3 27.2 reduce-scatter.4
  499.2 26.6 reduce-scatter.2
where the time goes:
time: 535 us
  waiting for transfers between devices  391 us (73%)
  blocking collectives  69.1 us (13%)
  other arithmetic  24.9 us (5%)
  matrix products  16.1 us (3%)
  starting transfers between devices  14 us (3%)
  between operations  13.9 us (3%)
  local copies, waits for them, and re-layouts  5.76 us (1%)
    psum x2, waiting for transfers between devices, masked_total(): summed = lax.psum(partial_value, ('layer', 'latent'))  326 us
    all_to_all x1, blocking collectives, body(): lax.all_to_all(enc_partial, 'latent', split_axis=0, concat_axis=1, tiled=...  40.9 us
    all_to_all x1, waiting for transfers between devices, body(): lax.all_to_all(dec_partial, 'latent', split_axis=0, concat_axis=1, tiled=...  35.6 us
    reduce_scatter x1, waiting for transfers between devices, body(): lax.psum_scatter(exchanged[0], 'token', scatter_dimension=1, tiled=True)  23.5 us
    reduce_sum x1, other arithmetic, body(): jnp.sum(matches(active_latents, total_lat).astype(jnp.float32), axis=1)  17.8 us
    all_gather x1, blocking collectives, body(): lax.all_gather(casted[1], 'token', axis=1, tiled=True)  14.4 us
    all_gather x1, blocking collectives, body(): lax.all_gather(casted[0], 'token', axis=1, tiled=True)  13.8 us
    dot_general x4, matrix products, contract(): lax.dot_general(left, right, (((left_dim,), (right_dim,)), ((), ())), pre...  13 us
  transfers between devices with their start and end apart: 7, of which 5 were waited for; matrix products, arithmetic and copies ran while one was open for 7% of the time, Pallas kernels for 0%

commit v1 on v0

--- a/solution.py
+++ b/solution.py
@@ -67,7 +67,12 @@
     enc_partial = contract(backward, own_rows, 0, 0) * (enc_scale / tokens_all)
     exchanged = (
         lax.all_to_all(enc_partial, "latent", split_axis=0, concat_axis=1, tiled=True),
-        lax.all_to_all(dec_partial, "latent", split_axis=0, concat_axis=1, tiled=True),
+        jnp.concatenate(
+            lax.all_to_all(
+                jnp.stack(jnp.split(dec_partial, lax.axis_size("latent"), axis=0)), "latent", 0, 0
+            ),
+            axis=1,
+        ),
     )
     enc_grad, dec_grad = (
         lax.psum_scatter(exchanged[0], "token", scatter_dimension=1, tiled=True),

time: 535 us -> 540 us (level)
  local copies, waits for them, and re-layouts: 5.76 us -> 11.6 us
where the time goes in v1:
time: 540 us; the launch traced here: 539 us
  waiting for transfers between devices  391 us (72%)
  blocking collectives  69.1 us (13%)
  other arithmetic  24.9 us (5%)
  matrix products  14.9 us (3%)
  starting transfers between devices  14 us (3%)
  between operations  13.9 us (3%)
  local copies, waits for them, and re-layouts  11.6 us (2%)
    psum x2, waiting for transfers between devices, masked_total(): summed = lax.psum(partial_value, ('layer', 'latent'))  326 us
    all_to_all x1, blocking collectives, body(): lax.all_to_all(enc_partial, 'latent', split_axis=0, concat_axis=1, tiled=...  40.9 us
    all_to_all x1, waiting for transfers between devices, body(): lax.all_to_all(jnp.stack(jnp.split(dec_partial, lax.axis_size('latent'),...  35.7 us
    reduce_scatter x1, waiting for transfers between devices, body(): lax.psum_scatter(exchanged[0], 'token', scatter_dimension=1, tiled=True)  23.5 us
    reduce_sum x1, other arithmetic, body(): jnp.sum(matches(active_latents, total_lat).astype(jnp.float32), axis=1)  17.8 us
    all_gather x1, blocking collectives, body(): lax.all_gather(casted[1], 'token', axis=1, tiled=True)  14.4 us
    all_gather x1, blocking collectives, body(): lax.all_gather(casted[0], 'token', axis=1, tiled=True)  13.8 us
    dot_general x4, matrix products, contract(): lax.dot_general(left, right, (((left_dim,), (right_dim,)), ((), ())), pre...  11.8 us
  transfers between devices with their start and end apart: 7, of which 5 were waited for; matrix products, arithmetic and copies ran while one was open for 7% of the time, Pallas kernels for 0%

profile of v1, /device:TPU:2, one launch (start us, length us, event | category | flops | bytes accessed | tf_op | source)
XLA Modules:
  0.0 539.4 jit_solution(18031079360154215731)
XLA Ops:
  7.2 1.0 bitcast_convert_fusion.1
  8.2 13.8 %all_gather.6 = bf16[48,8192]{1,0:T(8,128)(2,1)S(1)} all-gather(bf16[48,2048]{1,0:T(8,128)(2,1)S(1)} %bitcast_convert_fusion.1), channel_id=1, replica_groups=mesh['layer'=8,'latent'=8,'token'=4] {'token'}, dimensions={1}, use_global_device_ids=true | all-gather | bytes 983040 | tf_op jit(solution)/shard_map/all_gather | solution.py:51
  22.0 0.0 copy-start.8
  22.0 1.0 copy.41
  23.0 0.0 copy-start.2
  23.0 6.0 %all-to-all-start = ((bf16[48,8,1024]{2,0,1:T(8,128)(2,1)}), bf16[48,8,1024]{2,0,1:T(8,128)(2,1)}, u32[]{:S(2)}, u32[]{:S(2)}) async-start(bf16[48,8,1024]{2,0,1:T(8,128)(2,1)} %bitcast.115), calls=%async_computation | async-start | bytes 1572864 | tf_op jit(solution)/shard_map/all_to_all | solution.py:55
  29.0 0.0 copy-done.8
  29.0 0.2 copy.30
  29.2 0.0 copy-done.2
  29.3 14.4 %all_gather.7 = bf16[48,8192]{1,0:T(8,128)(2,1)S(1)} all-gather(bf16[48,2048]{1,0:T(8,128)(2,1)S(1)} %bitcast_convert_fusion), channel_id=1, replica_groups=mesh['layer'=8,'latent'=8,'token'=4] {'token'}, dimensions={1}, use_global_device_ids=true | all-gather | bytes 983040 | tf_op jit(solution)/shard_map/all_gather | solution.py:52
  43.7 0.0 copy-start
  43.7 1.0 copy.40
  44.7 5.4 %all-to-all-done = bf16[48,8,1024]{2,0,1:T(8,128)(2,1)} async-done(((bf16[48,8,1024]{2,0,1:T(8,128)(2,1)}), bf16[48,8,1024]{2,0,1:T(8,128)(2,1)}, u32[]{:S(2)}, u32[]{:S(2)}) %all-to-all-start) | async-done | bytes 786464 | tf_op jit(solution)/shard_map/all_to_all | solution.py:55
  50.1 4.2 all-to-all-start.1
  54.3 0.0 all-reduce.3.cloned.1.call-start
  54.4 0.0 copy-done
  54.4 3.5 fusion.4
  57.9 0.0 all-reduce.3.cloned.1.call-update
  58.0 17.8 %convert_reduce_fusion = f32[1024,384]{1,0:T(8,128)S(1)} fusion(s32[1024,64]{1,0:T(8,128)S(1)} %copy.30), kind=kLoop, calls=%fused_computation | loop fusion | flops 75104256 | bytes 1835008 | tf_op jit(solution)/shard_map/reduce_sum | solution.py:59
  75.8 172.1 %all-reduce.3.cloned.1.call-done = f32[1024,384]{1,0:T(8,128)} async-done(((f32[1024,384]{1,0:T(8,128)}), f32[1024,384]{1,0:T(8,128)}) %all-reduce.3.cloned.1.call-update) | async-done | bytes 1572880 | tf_op jit(solution)/shard_map/psum | solution.py:34
  247.8 1.6 multiply_convert_fusion.1
  249.4 0.0 all-to-all-done.1
  249.4 3.1 subtract_convert_fusion
  252.5 0.0 copy-start.1
  252.5 1.0 convolution_multiply_fusion
  253.5 0.3 copy-done.1
  253.8 0.7 fusion.21
  254.5 0.7 fusion.20
  255.2 0.7 fusion.19
  255.9 0.7 fusion.18
  256.6 0.7 fusion.17
  257.3 0.7 fusion.16
  258.0 0.7 fusion.15
  258.7 0.7 fusion.14
  259.3 3.6 all-to-all-start.3
  262.9 0.0 all-reduce.5.cloned.1.call-start
  263.0 4.2 convolution_multiply_fusion.1
  267.2 0.0 all-reduce.5.cloned.1.call-update
  267.2 0.0 reduce-scatter.5.cloned.1.call-start
  267.3 35.7 %all-to-all-done.3 = f32[8,48,1024]{2,1,0:T(8,128)S(1)} async-done(((f32[8,48,1024]{2,1,0:T(8,128)}), f32[8,48,1024]{2,1,0:T(8,128)S(1)}, u32[]{:S(2)}, u32[]{:S(2)}) %all-to-all-start.3) | async-done | bytes 1572896 | tf_op jit(solution)/shard_map/all_to_all | solution.py:71
  302.9 1.3 copy.37
  304.2 0.0 reduce-scatter.5.cloned.1.call-update
  304.2 0.0 reduce-scatter.3.cloned.1.call-start
  304.3 154.2 %all-reduce.5.cloned.1.call-done = f32[1024,384]{1,0:T(8,128)} async-done(((f32[1024,384]{1,0:T(8,128)}), f32[1024,384]{1,0:T(8,128)}) %all-reduce.5.cloned.1.call-update) | async-done | bytes 1572880 | tf_op jit(solution)/shard_map/psum | solution.py:34
  458.5 3.1 fusion.7
  461.5 40.9 %all_to_all.62 = f32[8,48,1024]{2,1,0:T(8,128)S(1)} all-to-all(f32[8,48,1024]{2,1,0:T(8,128)S(1)} %bitcast.120), channel_id=1, replica_groups=mesh['layer'=8,'latent'=8,'token'=4] {'latent'}, dimensions={0} | all-to-all | bytes 3145728 | tf_op jit(solution)/shard_map/all_to_all | solution.py:69
  502.4 1.3 copy.36
  503.7 0.0 copy-start.4
  503.7 0.0 copy-start.5
  503.7 0.0 reduce-scatter.3.cloned.1.call-update
  503.7 0.0 copy-start.3
  503.7 0.0 copy-start.6
  503.8 0.0 copy-start.7
  503.8 0.0 reduce-scatter.5.cloned.1.call-done
  503.8 0.9 copy-done.4
  504.7 0.1 copy-done.5
  504.8 2.2 fusion.24
  507.1 23.5 %reduce-scatter.3.cloned.1.call-done = f32[48,2048]{1,0:T(8,128)} async-done(((f32[48,8192]{1,0:T(8,128)}), f32[48,2048]{1,0:T(8,128)}) %reduce-scatter.3.cloned.1.call-update) | async-done | bytes 393232 | tf_op jit(solution)/shard_map/reduce_scatter | solution.py:78
  530.6 0.0 copy-done.3
  530.6 0.0 copy-done.6
  530.6 0.0 copy-done.7
  530.6 2.3 fusion.25
  (1 shorter events, 0.0 us)
Async XLA Ops:
  22.0 7.0 %copy-start.8 = (s32[1024,64]{0,1:T(8,128)S(1)}, s32[1024,64]{0,1:T(8,128)}, u32[]{:S(2)}) copy-start(s32[1024,64]{0,1:T(8,128)} %param.9) | copy-start | bytes 786436
  23.0 6.2 %copy-start.2 = (f32[1,48,2048]{2,1,0:T(8,128)S(1)}, f32[1,48,2048]{2,1,0:T(8,128)}, u32[]{:S(2)}) copy-start(f32[1,48,2048]{2,1,0:T(8,128)} %param.13) | copy-start | bytes 1179652
  23.0 27.1 %all-to-all-start = ((bf16[48,8,1024]{2,0,1:T(8,128)(2,1)}), bf16[48,8,1024]{2,0,1:T(8,128)(2,1)}, u32[]{:S(2)}, u32[]{:S(2)}) async-start(bf16[48,8,1024]{2,0,1:T(8,128)(2,1)} %bitcast.115), calls=%async_computation | async-start | bytes 1572864 | tf_op jit(solution)/shard_map/all_to_all | solution.py:55
  43.7 10.7 %copy-start = (bf16[1,1024,1024]{2,1,0:T(8,128)(2,1)S(1)}, bf16[1,1024,1024]{2,1,0:T(8,128)(2,1)}, u32[]{:S(2)}) copy-start(bf16[1,1024,1024]{2,1,0:T(8,128)(2,1)} %param.8) | copy-start | bytes 6291460
  50.1 199.3 %all-to-all-start.1 = ((bf16[48,8,1024]{2,0,1:T(8,128)(2,1)}), bf16[48,8,1024]{2,0,1:T(8,128)(2,1)}, u32[]{:S(2)}, u32[]{:S(2)}) async-start(bf16[48,8,1024]{2,0,1:T(8,128)(2,1)} %bitcast.114), calls=%async_computation.1 | async-start | bytes 1572864 | tf_op jit(solution)/shard_map/all_to_all | solution.py:56
  54.3 193.5 %all-reduce.3.cloned.1.call-start = ((), (), s32[]{:S(2)}) async-start(), calls=%async_computation.6 | async-start | bytes 3145728 | tf_op jit(solution)/shard_map/psum | solution.py:34
  252.5 1.3 copy-start.1
  259.3 43.6 %all-to-all-start.3 = ((f32[8,48,1024]{2,1,0:T(8,128)}), f32[8,48,1024]{2,1,0:T(8,128)S(1)}, u32[]{:S(2)}, u32[]{:S(2)}) async-start(f32[8,48,1024]{2,1,0:T(8,128)} %fusion.14), calls=%async_computation.4 | async-start | bytes 3145728 | tf_op jit(solution)/shard_map/all_to_all | solution.py:71
  262.9 195.5 %all-reduce.5.cloned.1.call-start = ((), (), s32[]{:S(2)}) async-start(), calls=%async_computation.7 | async-start | bytes 3145728 | tf_op jit(solution)/shard_map/psum | solution.py:34
  267.2 236.6 %reduce-scatter.5.cloned.1.call-start = ((), (), s32[]{:S(2)}) async-start(), calls=%async_computation.9 | async-start | bytes 1966080 | tf_op jit(solution)/shard_map/reduce_scatter | solution.py:79
  304.2 226.3 %reduce-scatter.3.cloned.1.call-start = ((), (), s32[]{:S(2)}) async-start(), calls=%async_computation.8 | async-start | bytes 1966080 | tf_op jit(solution)/shard_map/reduce_scatter | solution.py:78
  503.7 1.0 copy-start.4
  503.7 1.1 copy-start.5
  503.7 26.9 %copy-start.3 = (f32[1,48,2048]{2,1,0:T(8,128)S(1)}, f32[1,48,2048]{2,1,0:T(8,128)}, u32[]{:S(2)}) copy-start(f32[1,48,2048]{2,1,0:T(8,128)} %param.10) | copy-start | bytes 1179652
  503.7 26.8 %copy-start.6 = (f32[1,48,2048]{2,1,0:T(8,128)S(1)}, f32[1,48,2048]{2,1,0:T(8,128)}, u32[]{:S(2)}) copy-start(f32[1,48,2048]{2,1,0:T(8,128)} %param.12) | copy-start | bytes 1179652
  503.8 26.8 %copy-start.7 = (f32[1,48,2048]{2,1,0:T(8,128)S(1)}, f32[1,48,2048]{2,1,0:T(8,128)}, u32[]{:S(2)}) copy-start(f32[1,48,2048]{2,1,0:T(8,128)} %param.11) | copy-start | bytes 1179652
Sparse Core Ops, SparseCore 0:
  58.6 189.2 all-reduce.2
  267.3 191.0 all-reduce.4
  461.0 27.2 reduce-scatter.4
  503.8 26.6 reduce-scatter.2
